TPU v7x, 256 devices: a whole 4x4x8 slice. The times are simulated.
256 devices in a mesh: member: 4 (over y), slab: 2 (over core), tile: 32 (over x, z).
Axes of the slice: x: 4, y: 4, z: 8, core: 2. Of those that a mesh axis runs over, the one named last changes fastest.
Arguments:
- prior: float32 [128, 262144], P('member', ('slab', 'tile')), may hold values from -6 to 6
- sensitivity: bfloat16 [512, 16, 64, 512], P(('slab', 'tile')), may hold values from -0.0625 to 0.0625
- pattern: int32 [512, 16], P(('slab', 'tile')), may hold values from -1 to 511, as said below
- ownership: int32 [512], replicated, may hold values from 0 to 511, each once
- observed: float32 [32768], P(('slab', 'tile')), may hold values from -8 to 8
- obs_noise: float32 [32768], P(('slab', 'tile')), may hold values from 0.3 to 3
- perturbation: float32 [128, 32768], P('member', ('slab', 'tile')), may hold values from -5 to 5
Outputs:
- increment: float32 [128, 262144], P('member', ('slab', 'tile'))
- weights: float32 [128, 128], replicated
Inputs may be any that keep to these rules, and one draw needn't show every extreme that they name: In each row of pattern the first c entries are distinct observation block numbers and the remaining 16 - c entries are -1, with 4 <= c <= 16; some row is full and some row has exactly 4 live entries.
All inputs are finite; a program needn't handle non-finite values.
Results may differ from a plain program's by a relative error of at most 0.0042.
Values may be sent and summed in bfloat16 or wider, within the bound.
A program may use at most 64 MiB of HBM per device.

v0:
```python
import math
import jax
import jax.numpy as jnp
from jax import lax
from jax.sharding import PartitionSpec as P


def local(prior, sensitivity, pattern, ownership, observed, obs_noise, perturbation):
    members_dev = prior.shape[0]
    members = members_dev * lax.axis_size("member")
    blocks_dev = sensitivity.shape[0]
    slot_count = sensitivity.shape[1]
    obs_block = sensitivity.shape[2]
    block_total = ownership.shape[0]
    obs_dev = observed.shape[0]
    owned_blocks = obs_dev // obs_block
    norm_scale = 1.0 / math.sqrt(members - 1)
    prior_bf = prior.astype(jnp.bfloat16)
    shaped = prior_bf.reshape(members_dev, blocks_dev, sensitivity.shape[3])
    contrib = jnp.einsum("bkop,mbp->bkmo", sensitivity, shaped, preferred_element_type=jnp.float32)
    contrib_rows = contrib.reshape(blocks_dev * slot_count, members_dev * obs_block)
    flat_pattern = pattern.reshape(blocks_dev * slot_count)
    storage_of = (
        jnp.zeros((block_total,), jnp.int32)
        .at[ownership]
        .set(jnp.arange(block_total, dtype=jnp.int32))
    )
    slot_rows = jnp.where(flat_pattern >= 0, storage_of[jnp.maximum(flat_pattern, 0)], block_total)
    local_rows = slot_rows - 0
    target = jnp.where((local_rows >= 0) & (local_rows < block_total), local_rows, block_total)
    placed = (
        jnp.zeros((block_total + 1, members_dev * obs_block), jnp.float32)
        .at[target]
        .add(contrib_rows)
    )
    summed = lax.psum(placed[:block_total], ("slab", "tile"))
    owned_rows = lax.dynamic_slice_in_dim(
        summed, lax.axis_index(("slab", "tile")) * owned_blocks, owned_blocks, 0
    )
    predicted = (
        owned_rows.reshape(owned_blocks, members_dev, obs_block)
        .transpose(1, 0, 2)
        .reshape(members_dev, obs_dev)
    )
    mean_pred = lax.psum(jnp.sum(predicted, axis=0), "member") / members
    spread = (predicted - mean_pred) * norm_scale / obs_noise
    innovation = (observed - predicted) / obs_noise + perturbation
    spread_all, innov_all = (
        lax.all_gather(spread, "member", axis=0, tiled=True),
        lax.all_gather(innovation, "member", axis=0, tiled=True),
    )
    gram_local = jnp.einsum("mo,ko->mk", spread_all, spread_all, precision=lax.Precision.HIGHEST)
    cross_local = jnp.einsum("mo,ko->mk", spread_all, innov_all, precision=lax.Precision.HIGHEST)
    misfit_local = jnp.sum(innov_all * innov_all)
    gram_matrix, cross_term, misfit = lax.psum(
        (gram_local, cross_local, misfit_local), ("slab", "tile")
    )
    damping = misfit / (4.0 * members * members)
    system = gram_matrix + damping * jnp.eye(members, dtype=jnp.float32)
    factor = jnp.linalg.cholesky(system)
    weights = jax.scipy.linalg.cho_solve((factor, True), cross_term)
    centred = ((weights - jnp.mean(weights, axis=0, keepdims=True)) * norm_scale).astype(
        jnp.bfloat16
    )
    member_start = lax.axis_index("member") * members_dev
    own_cols = lax.dynamic_slice_in_dim(centred, member_start, members_dev, 1)
    increment = lax.dot_general(
        own_cols,
        lax.all_gather(prior_bf, "member", axis=0, tiled=True),
        (((0,), (0,)), ((), ())),
        preferred_element_type=jnp.float32,
    )
    return (increment, weights)


def solution(mesh):
    return jax.shard_map(
        local,
        mesh=mesh,
        in_specs=(
            P("member", ("slab", "tile")),
            P(("slab", "tile"), None, None, None),
            P(("slab", "tile"), None),
            P(),
            P(("slab", "tile")),
            P(("slab", "tile")),
            P("member", ("slab", "tile")),
        ),
        out_specs=(P("member", ("slab", "tile")), P()),
        check_vma=False,
    )
```

profile of v0, /device:TPU:1, one launch (start us, length us, event | category | flops | bytes accessed | tf_op | source)
XLA Modules:
  0.0 477.4 jit_solution(6537073593213794000)
XLA Ops:
  8.0 0.0 all-reduce.4.cloned.1.call-start
  8.0 0.7 broadcast_maximum_fusion
  8.7 0.7 broadcast_compare_fusion
  9.4 1.1 convert_element_type.7
  10.5 0.0 copy-start
  10.5 0.1 copy.22
  10.6 0.0 copy-start.4
  10.6 7.3 %convolution_bitcast_fusion = f32[8,16,32,64]{3,2,1,0:T(8,128)S(1)} fusion(bf16[8,16,64,512]{3,2,1,0:T(8,128)(2,1)} %param.8, bf16[32,8,512,1]{2,1,0,3:T(8,128)(2,1)S(1)} %bitcast.39), kind=kOutput, calls=%fused_computation.5 | convolution fusion | flops 268435456 | bytes 9699328 | tf_op jit(solution)/shard_map/bkop,mbp->bkmo/dot_general | solution.py:20
  18.0 0.0 copy-done
  18.0 0.7 reshape.114
  18.6 0.1 reshape.96
  18.7 0.0 copy-done.4
  18.7 0.1 ge.26
  18.8 2.4 scatter_custom_fusion
  21.3 1.3 gather_fusion
  22.6 4.3 scatter_custom_fusion.1
  26.9 4.7 slice.24
  31.6 0.0 all-reduce.4.cloned.1.call-update
  31.6 0.0 all-reduce.6.cloned.1.call-start
  31.6 197.7 %all-reduce.4.cloned.1.call-done = f32[512,2048]{1,0:T(8,128)} async-done(((f32[512,2048]{1,0:T(8,128)}), f32[512,2048]{1,0:T(8,128)}) %all-reduce.4.cloned.1.call-update) | async-done | bytes 4194320 | tf_op jit(solution)/shard_map/psum | solution.py:36
  229.3 0.8 constant_dynamic-slice_fusion
  230.2 0.1 reshape.92
  230.3 0.1 copy.16
  230.4 0.1 reshape.93
  230.5 0.1 reduce_sum.30
  230.5 8.4 %psum.36 = f32[512]{0:T(512)S(1)} all-reduce(f32[512]{0:T(512)S(1)} %reduce_sum.30), channel_id=1, replica_groups=mesh['member'=4,'slab'=2,'tile'=32] {'member'}, use_global_device_ids=true, to_apply=%region_4.5 | all-reduce | flops 512 | bytes 4096 | tf_op jit(solution)/shard_map/psum | solution.py:45
  239.0 10.0 %all_gather.10 = f32[128,512]{1,0:T(8,128)S(1)} all-gather(f32[32,512]{1,0:T(8,128)S(1)} %get-tuple-element.10), channel_id=1, replica_groups=mesh['member'=4,'slab'=2,'tile'=32] {'member'}, dimensions={0}, use_global_device_ids=true | all-gather | bytes 327680 | tf_op jit(solution)/shard_map/all_gather | solution.py:50
  249.0 9.4 %all_gather.9 = f32[128,512]{1,0:T(8,128)S(1)} all-gather(f32[32,512]{1,0:T(8,128)S(1)} %get-tuple-element.11), channel_id=1, replica_groups=mesh['member'=4,'slab'=2,'tile'=32] {'member'}, dimensions={0}, use_global_device_ids=true | all-gather | bytes 327680 | tf_op jit(solution)/shard_map/all_gather | solution.py:49
  258.4 1.0 fusion.21
  259.4 1.0 fusion.22
  260.4 0.0 all-reduce.6.cloned.1.call-update
  260.4 0.0 all-gather.2.cloned.1.call-start
  260.5 0.5 all-gather.2.cloned.1.call-update
  261.0 0.7 multiply_reduce_fusion
  261.6 135.2 %psum.38 = f32[]{:T(128)} all-reduce(f32[]{:T(128)} %multiply_reduce_fusion), channel_id=1, replica_groups=mesh['member'=4,'slab'=2,'tile'=32] {'slab','tile'}, use_global_device_ids=true, to_apply=%region_7.8 | all-reduce | flops 1 | bytes 8 | tf_op jit(solution)/shard_map/psum | solution.py:55
  397.4 43.2 %all-reduce.6.cloned.1.call-done = (f32[128,128]{1,0:T(8,128)}, f32[128,128]{1,0:T(8,128)}) async-done(((f32[128,128]{1,0:T(8,128)}, f32[128,128]{1,0:T(8,128)}), (f32[128,128]{1,0:T(8,128)}, f32[128,128]{1,0:T(8,128)})) %all-reduce.6.cloned.1.call-update) | async-done | bytes 131088 | tf_op jit(solution)/shard_map/psum | solution.py:55
  440.6 0.9 select_add_fusion
  441.5 0.1 copy.17
  441.6 0.9 fusion.8
  442.5 11.7 %cholesky.16 = f32[128,128]{1,0:T(8,128)S(1)} custom-call(f32[128,128]{1,0:T(8,128)S(1)} %fusion.8), custom_call_target="Cholesky" | custom-call | tf_op jit(solution)/shard_map/jit(cholesky)/cholesky | solution.py:60
  454.2 0.6 compare_reduce_fusion
  454.9 0.7 fusion.3
  455.5 9.8 %custom-call.10 = f32[1,128,128]{1,2,0:T(8,128)S(1)} custom-call(f32[1,128,128]{2,1,0:T(8,128)S(1)} %fusion.3), custom_call_target="InvertDiagBlocksLowerTriangular" | custom-call | tf_op jit(solution)/shard_map/jit(_cho_solve)/triangular_solve | solution.py:61
  465.3 1.1 fusion.6
  466.5 0.4 fusion.20
  466.8 0.7 copy.18
  467.6 0.1 dynamic-slice
  467.7 2.3 fusion.11
  (16 shorter events, 0.1 us)
Async XLA Ops:
  8.0 221.3 %all-reduce.4.cloned.1.call-start = ((), (), s32[]{:S(2)}) async-start(), calls=%async_computation | async-start | bytes 8388608 | tf_op jit(solution)/shard_map/psum | solution.py:36
  10.5 7.5 %copy-start = (bf16[32,4096]{1,0:T(8,128)(2,1)}, bf16[32,4096]{1,0:T(8,128)(2,1)S(1)}, u32[]{:S(2)}) copy-start(bf16[32,4096]{1,0:T(8,128)(2,1)S(1)} %convert_element_type.7) | copy-start | bytes 786436
  10.6 8.1 %copy-start.4 = (s32[512]{0:T(512)S(1)}, s32[512]{0:T(512)}, u32[]{:S(2)}) copy-start(s32[512]{0:T(512)} %param.10) | copy-start | bytes 6148
  31.5 207.4 %copy-start.1 = (f32[32,512]{1,0:T(8,128)S(1)}, f32[32,512]{1,0:T(8,128)}, u32[]{:S(2)}) copy-start(f32[32,512]{1,0:T(8,128)} %param.13) | copy-start | bytes 196612
  31.5 207.4 %copy-start.2 = (f32[512]{0:T(512)S(1)}, f32[512]{0:T(512)}, u32[]{:S(2)}) copy-start(f32[512]{0:T(512)} %param.11) | copy-start | bytes 6148
  31.5 207.4 %copy-start.3 = (f32[512]{0:T(512)S(1)}, f32[512]{0:T(512)}, u32[]{:S(2)}) copy-start(f32[512]{0:T(512)} %param.12) | copy-start | bytes 6148
  31.6 409.1 %all-reduce.6.cloned.1.call-start = ((), (), s32[]{:S(2)}) async-start(), calls=%async_computation.2 | async-start | bytes 262144 | tf_op jit(solution)/shard_map/psum | solution.py:55
  260.4 207.2 %all-gather.2.cloned.1.call-start = ((), (), s32[]{:S(2)}) async-start(), calls=%async_computation.1 | async-start | bytes 1310720 | tf_op jit(solution)/shard_map/all_gather | solution.py:69
Sparse Core Ops, SparseCore 0:
  31.7 197.5 all-reduce.3
  260.5 180.0 all-reduce.5
Sparse Core Ops, SparseCore 1:
  263.3 31.1 all-gather.1
where the time goes:
time: 478 us; the launch traced here: 477 us
  waiting for transfers between devices  241 us (50%)
  blocking collectives  163 us (34%)
  other arithmetic  32.1 us (7%)
  between operations  16.2 us (3%)
  matrix products  13.2 us (3%)
  local copies, waits for them, and re-layouts  11.4 us (2%)
    psum x1, waiting for transfers between devices, local(): summed = lax.psum(placed[:block_total], ('slab', 'tile'))  198 us
    psum x1, blocking collectives, local(): lax.psum((gram_local, cross_local, misfit_local), ('slab', 'tile'))  135 us
    psum x1, waiting for transfers between devices, local(): lax.psum((gram_local, cross_local, misfit_local), ('slab', 'tile'))  43.2 us
    another operation x3, other arithmetic, local(): factor = jnp.linalg.cholesky(system)  12.4 us
    another operation x2, other arithmetic, local(): weights = jax.scipy.linalg.cho_solve((factor, True), cross_term)  10.5 us
    all_gather x1, blocking collectives, local(): lax.all_gather(innovation, 'member', axis=0, tiled=True)  10 us
  transfers between devices with their start and end apart: 3, of which 2 were waited for; matrix products, arithmetic and copies ran while one was open for 6% of the time, Pallas kernels for 0%

commit v1 on v0

--- a/solution.py
+++ b/solution.py
@@ -3,6 +3,27 @@
 import jax.numpy as jnp
 from jax import lax
 from jax.sharding import PartitionSpec as P
+
+
+def collect(array, axis, dim):
+    size, position, extent = (lax.axis_size(axis), lax.axis_index(axis), array.shape[dim])
+    ahead = [(i, (i + 1) % size) for i in range(size)]
+    left = [(i, (i - 1) % size) for i in range(size)]
+    out = jnp.zeros((*array.shape[:dim], size * extent, *array.shape[dim + 1 :]), array.dtype)
+    out = lax.dynamic_update_slice_in_dim(out, array, position * extent, axis=dim)
+    from_left = from_right = array
+    half = size // 2
+    for hop in range(1, half + 1):
+        from_left = lax.ppermute(from_left, axis, ahead)
+        out = lax.dynamic_update_slice_in_dim(
+            out, from_left, (position - hop) % size * extent, axis=dim
+        )
+        if hop < size - half:
+            from_right = lax.ppermute(from_right, axis, left)
+            out = lax.dynamic_update_slice_in_dim(
+                out, from_right, (position + hop) % size * extent, axis=dim
+            )
+    return out
 
 
 def local(prior, sensitivity, pattern, ownership, observed, obs_noise, perturbation):
@@ -47,7 +68,7 @@
     innovation = (observed - predicted) / obs_noise + perturbation
     spread_all, innov_all = (
         lax.all_gather(spread, "member", axis=0, tiled=True),
-        lax.all_gather(innovation, "member", axis=0, tiled=True),
+        collect(innovation, "member", 0),
     )
     gram_local = jnp.einsum("mo,ko->mk", spread_all, spread_all, precision=lax.Precision.HIGHEST)
     cross_local = jnp.einsum("mo,ko->mk", spread_all, innov_all, precision=lax.Precision.HIGHEST)

time: 478 us -> 473 us (0.990)
  blocking collectives: 163 us -> 152 us
    all_gather x1 -> x0, blocking collectives: 10 us -> none  [local(): lax.all_gather(innovation, 'member', axis=0, tiled=True)]
  transfers between devices with their start and end apart: 3 -> 6, of which waited for: 2 -> 3; matrix products, arithmetic and copies ran while one was open for 6% -> 6% of each run, Pallas kernels for 0% -> 0%
where the time goes in v1:
time: 473 us
  waiting for transfers between devices  245 us (52%)
  blocking collectives  152 us (32%)
  other arithmetic  32.1 us (7%)
  between operations  16.3 us (3%)
  matrix products  13.2 us (3%)
  local copies, waits for them, and re-layouts  11.4 us (2%)
    psum x1, waiting for transfers between devices, local(): summed = lax.psum(placed[:block_total], ('slab', 'tile'))  198 us
    psum x1, blocking collectives, local(): lax.psum((gram_local, cross_local, misfit_local), ('slab', 'tile'))  135 us
    psum x1, waiting for transfers between devices, local(): lax.psum((gram_local, cross_local, misfit_local), ('slab', 'tile'))  42.7 us
    another operation x3, other arithmetic, local(): factor = jnp.linalg.cholesky(system)  12.4 us
    another operation x2, other arithmetic, local(): weights = jax.scipy.linalg.cho_solve((factor, True), cross_term)  10.5 us
  transfers between devices with their start and end apart: 6, of which 3 were waited for; matrix products, arithmetic and copies ran while one was open for 6% of the time, Pallas kernels for 0%

profile of v1, /device:TPU:1, one launch (start us, length us, event | category | flops | bytes accessed | tf_op | source)
XLA Modules:
  0.0 472.9 jit_solution(2316950823821924489)
XLA Ops:
  8.0 0.0 all-reduce.4.cloned.1.call-start
  8.0 0.7 broadcast_maximum_fusion
  8.7 0.7 broadcast_compare_fusion
  9.4 1.1 convert_element_type.7
  10.5 0.0 copy-start
  10.5 0.1 copy.22
  10.6 0.0 copy-start.4
  10.6 7.3 %convolution_bitcast_fusion = f32[8,16,32,64]{3,2,1,0:T(8,128)S(1)} fusion(bf16[8,16,64,512]{3,2,1,0:T(8,128)(2,1)} %param.8, bf16[32,8,512,1]{2,1,0,3:T(8,128)(2,1)S(1)} %bitcast.39), kind=kOutput, calls=%fused_computation.5 | convolution fusion | flops 268435456 | bytes 9699328 | tf_op jit(solution)/shard_map/bkop,mbp->bkmo/dot_general | solution.py:41
  18.0 0.7 reshape.114
  18.6 0.1 reshape.96
  18.7 0.1 ge.26
  18.8 2.4 scatter_custom_fusion
  21.3 1.3 gather_fusion
  22.6 4.3 scatter_custom_fusion.1
  26.9 4.7 slice.24
  31.6 0.0 all-reduce.4.cloned.1.call-update
  31.6 0.0 all-reduce.6.cloned.1.call-start
  31.7 197.6 %all-reduce.4.cloned.1.call-done = f32[512,2048]{1,0:T(8,128)} async-done(((f32[512,2048]{1,0:T(8,128)}), f32[512,2048]{1,0:T(8,128)}) %all-reduce.4.cloned.1.call-update) | async-done | bytes 4194320 | tf_op jit(solution)/shard_map/psum | solution.py:57
  229.3 0.8 constant_dynamic-slice_fusion
  230.2 0.1 reshape.92
  230.3 0.1 copy.16
  230.4 0.1 reshape.93
  230.5 0.1 reduce_sum.30
  230.5 8.4 %psum.36 = f32[512]{0:T(512)S(1)} all-reduce(f32[512]{0:T(512)S(1)} %reduce_sum.30), channel_id=1, replica_groups=mesh['member'=4,'slab'=2,'tile'=32] {'member'}, use_global_device_ids=true, to_apply=%region_4.5 | all-reduce | flops 512 | bytes 4096 | tf_op jit(solution)/shard_map/psum | solution.py:66
  239.0 0.1 collective-permute-start
  239.1 2.7 collective-permute-start.1
  241.8 9.4 %all_gather.6 = f32[128,512]{1,0:T(8,128)S(1)} all-gather(f32[32,512]{1,0:T(8,128)S(1)} %get-tuple-element.12), channel_id=1, replica_groups=mesh['member'=4,'slab'=2,'tile'=32] {'member'}, dimensions={0}, use_global_device_ids=true | all-gather | bytes 327680 | tf_op jit(solution)/shard_map/all_gather | solution.py:70
  251.2 1.0 fusion.21
  252.2 4.3 collective-permute-done.2
  256.5 1.0 fusion.22
  257.5 0.0 all-reduce.6.cloned.1.call-update
  257.5 0.0 all-gather.2.cloned.1.call-start
  257.6 0.7 multiply_reduce_fusion
  258.2 0.0 all-gather.2.cloned.1.call-update
  258.3 134.6 %psum.38 = f32[]{:T(128)} all-reduce(f32[]{:T(128)} %multiply_reduce_fusion), channel_id=1, replica_groups=mesh['member'=4,'slab'=2,'tile'=32] {'slab','tile'}, use_global_device_ids=true, to_apply=%region_7.8 | all-reduce | flops 1 | bytes 8 | tf_op jit(solution)/shard_map/psum | solution.py:76
  393.4 42.7 %all-reduce.6.cloned.1.call-done = (f32[128,128]{1,0:T(8,128)}, f32[128,128]{1,0:T(8,128)}) async-done(((f32[128,128]{1,0:T(8,128)}, f32[128,128]{1,0:T(8,128)}), (f32[128,128]{1,0:T(8,128)}, f32[128,128]{1,0:T(8,128)})) %all-reduce.6.cloned.1.call-update) | async-done | bytes 131088 | tf_op jit(solution)/shard_map/psum | solution.py:76
  436.1 0.9 select_add_fusion
  437.0 0.1 copy.17
  437.1 0.9 fusion.8
  437.9 11.7 %cholesky.16 = f32[128,128]{1,0:T(8,128)S(1)} custom-call(f32[128,128]{1,0:T(8,128)S(1)} %fusion.8), custom_call_target="Cholesky" | custom-call | tf_op jit(solution)/shard_map/jit(cholesky)/cholesky | solution.py:81
  449.7 0.6 compare_reduce_fusion
  450.3 0.7 fusion.3
  451.0 9.8 %custom-call.10 = f32[1,128,128]{1,2,0:T(8,128)S(1)} custom-call(f32[1,128,128]{2,1,0:T(8,128)S(1)} %fusion.3), custom_call_target="InvertDiagBlocksLowerTriangular" | custom-call | tf_op jit(solution)/shard_map/jit(_cho_solve)/triangular_solve | solution.py:82
  460.8 1.1 fusion.6
  461.9 0.4 fusion.20
  462.3 0.1 dynamic-slice
  462.4 0.7 copy.18
  463.1 2.3 fusion.11
  (25 shorter events, 0.2 us)
Async XLA Ops:
  8.0 221.3 %all-reduce.4.cloned.1.call-start = ((), (), s32[]{:S(2)}) async-start(), calls=%async_computation | async-start | bytes 8388608 | tf_op jit(solution)/shard_map/psum | solution.py:57
  10.5 7.5 %copy-start = (bf16[32,4096]{1,0:T(8,128)(2,1)}, bf16[32,4096]{1,0:T(8,128)(2,1)S(1)}, u32[]{:S(2)}) copy-start(bf16[32,4096]{1,0:T(8,128)(2,1)S(1)} %convert_element_type.7) | copy-start | bytes 786436
  10.6 8.1 %copy-start.4 = (s32[512]{0:T(512)S(1)}, s32[512]{0:T(512)}, u32[]{:S(2)}) copy-start(s32[512]{0:T(512)} %param.10) | copy-start | bytes 6148
  31.5 207.4 %copy-start.1 = (f32[32,512]{1,0:T(8,128)S(1)}, f32[32,512]{1,0:T(8,128)}, u32[]{:S(2)}) copy-start(f32[32,512]{1,0:T(8,128)} %param.13) | copy-start | bytes 196612
  31.5 207.4 %copy-start.2 = (f32[512]{0:T(512)S(1)}, f32[512]{0:T(512)}, u32[]{:S(2)}) copy-start(f32[512]{0:T(512)} %param.12) | copy-start | bytes 6148
  31.5 207.5 %copy-start.3 = (f32[512]{0:T(512)S(1)}, f32[512]{0:T(512)}, u32[]{:S(2)}) copy-start(f32[512]{0:T(512)} %param.11) | copy-start | bytes 6148
  31.6 404.5 %all-reduce.6.cloned.1.call-start = ((), (), s32[]{:S(2)}) async-start(), calls=%async_computation.2 | async-start | bytes 262144 | tf_op jit(solution)/shard_map/psum | solution.py:76
  239.0 13.1 %collective-permute-start = (f32[32,512]{1,0:T(8,128)S(1)}, f32[32,512]{1,0:T(8,128)S(1)}, u32[]{:S(2)}, u32[]{:S(2)}) collective-permute-start(f32[32,512]{1,0:T(8,128)S(1)} %get-tuple-element.11), channel_id=1, source_target_pairs={{0,64},{64,128},{128,192},{192,0},{1,65},{65,129},{129,193},{193,1... | collective-permute-start | bytes 196616 | tf_op jit(solution)/shard_map/ppermute | solution.py:17
  239.1 13.0 %collective-permute-start.1 = (f32[32,512]{1,0:T(8,128)S(1)}, f32[32,512]{1,0:T(8,128)S(1)}, u32[]{:S(2)}, u32[]{:S(2)}) collective-permute-start(f32[32,512]{1,0:T(8,128)S(1)} %get-tuple-element.11), channel_id=1, source_target_pairs={{0,192},{64,0},{128,64},{192,128},{1,193},{65,1},{129,65},{193,129... | collective-permute-start | bytes 196616 | tf_op jit(solution)/shard_map/ppermute | solution.py:22
  252.2 4.3 collective-permute-start.2
  257.5 205.6 %all-gather.2.cloned.1.call-start = ((), (), s32[]{:S(2)}) async-start(), calls=%async_computation.1 | async-start | bytes 1310720 | tf_op jit(solution)/shard_map/all_gather | solution.py:90
Sparse Core Ops, SparseCore 0:
  31.7 197.5 all-reduce.3
  257.7 178.4 all-reduce.5
Sparse Core Ops, SparseCore 1:
  260.4 29.4 all-gather.1
